TPU v7x, 256 devices: a whole 4x4x8 slice. The times are simulated.
256 devices in a mesh: tm: 16 (over x, y), space: 16 (over z, core).
Axes of the slice: x: 4, y: 4, z: 8, core: 2. Of those that a mesh axis runs over, the one named last changes fastest.
Arguments:
- queries: bfloat16 [32, 32, 32, 2240], P('tm', 'space'), may hold values from -6 to 6
- keys: bfloat16 [32, 32, 32, 2240], P('tm', 'space'), may hold values from -6 to 6
- values: bfloat16 [32, 32, 32, 2240], P('tm', 'space'), may hold values from -6 to 6
- out_grad: bfloat16 [32, 32, 32, 2240], P('tm', 'space'), may hold values from -6 to 6
- block_start: int32 [32], P('tm'), may hold values 0 or 1
- conv_input: bfloat16 [32, 32, 32, 5632], P('tm', 'space'), may hold values from -6 to 6
- conv_grad: bfloat16 [32, 32, 32, 5632], P('tm', 'space'), may hold values from -6 to 6
- conv_weight: float32 [9, 5632], replicated, may hold values from -2 to 2
Outputs:
- query_grad: bfloat16 [32, 32, 32, 2240], P('tm', 'space')
- key_grad: bfloat16 [32, 32, 32, 2240], P('tm', 'space')
- value_grad: bfloat16 [32, 32, 32, 2240], P('tm', 'space')
- input_grad: bfloat16 [32, 32, 32, 5632], P('tm', 'space')
- kernel_grad: float32 [9, 5632], replicated
All inputs are finite; a program needn't handle non-finite values. No bound on the sum of `block_start` on one device may be relied on, other than what follows from the above.
Results may differ from a plain program's by a relative error of at most 0.0088.
Values may be sent and summed in bfloat16 or wider, within the bound.
A program may use at most 128 MiB of HBM per device.

v0:
```python
import math
import jax
import jax.numpy as jnp
from jax import lax
from jax.sharding import PartitionSpec as P

HEADS = 20
HD = 112
highest = lax.Precision.HIGHEST


def with_halo(cells, sides, width):
    for axis, dim in sides:
        count = lax.axis_size(axis)
        ends = count - 1
        head = lax.slice_in_dim(cells, 0, width, axis=dim)
        tail = lax.slice_in_dim(cells, cells.shape[dim] - width, cells.shape[dim], axis=dim)
        cells = jnp.concatenate(
            [
                lax.ppermute(tail, axis, [(i, (i + 1) % count) for i in range(ends)]),
                cells,
                lax.ppermute(head, axis, [((i + 1) % count, i) for i in range(ends)]),
            ],
            axis=dim,
        )
    return cells


def prefix(part, axis, combine, identity, reverse):
    count = lax.axis_size(axis)
    place = lax.axis_index(axis)
    ahead = count - 1 - place if reverse else place
    gathered = jax.tree.map(lambda a: lax.all_gather(a, axis), part)
    state = jax.tree.map(lambda a, e: jnp.zeros_like(a) + jnp.asarray(e, a.dtype), part, identity)

    def one(turn, state):
        source = count - 1 - turn if reverse else turn
        return combine(
            state, jax.tree.map(lambda a: lax.dynamic_index_in_dim(a, source, 0, False), gathered)
        )

    return lax.fori_loop(0, ahead, one, state)


def lifted(x):
    widened = x.astype(jnp.float32)
    return jnp.where(widened > 0, widened + 1.0, jnp.exp(jnp.minimum(widened, 0.0)))


def slopes(x):
    widened = x.astype(jnp.float32)
    return jnp.where(widened > 0, 1.0, jnp.exp(jnp.minimum(widened, 0.0)))


def visibility(block_start, count):
    position = jnp.arange(count, dtype=jnp.int32)
    starts = jnp.where(position == 0, 1, block_start)
    block_ids = jnp.cumsum(starts)
    return (block_ids[None, :] <= block_ids[:, None]).astype(jnp.float32)


def add_pair(earlier, later):
    return (earlier[0] + later[0], earlier[1] + later[1])


def body(queries, keys, values, out_grad, block_start, conv_input, conv_grad, conv_weight):
    frames, rows, cols, width = queries.shape
    heads = HEADS
    depth = HD
    head_shape = (frames, rows * cols, heads, depth)
    q_feat = lifted(queries).astype(jnp.bfloat16).reshape(head_shape)
    k_feat = lifted(keys).astype(jnp.bfloat16).reshape(head_shape)
    v_heads = values.reshape(head_shape)
    visible = visibility(block_start, frames)
    rimmed = with_halo(conv_grad, (("space", 1),), 1)
    states = jnp.einsum("fnhd,fnhe->fhde", k_feat, v_heads, preferred_element_type=jnp.float32)
    sums = jnp.sum(k_feat.astype(jnp.float32), axis=1)
    states, sums = lax.psum((states, sums), "space")
    earlier = prefix(
        (jnp.sum(states, axis=0), jnp.sum(sums, axis=0)),
        "tm",
        add_pair,
        (jnp.zeros(states.shape[1:], jnp.float32), jnp.zeros(sums.shape[1:], jnp.float32)),
        False,
    )
    seen_states = jnp.einsum("fg,ghde->fhde", visible, states, precision=highest) + earlier[0][None]
    seen_sums = jnp.einsum("fg,ghd->fhd", visible, sums, precision=highest) + earlier[1][None]
    q_wide = q_feat.astype(jnp.float32)
    grad_wide = out_grad.reshape(head_shape).astype(jnp.float32)
    numer = jnp.einsum("fnhd,fhde->fnhe", q_wide, seen_states, precision=highest)
    denominator = jnp.einsum("fnhd,fhd->fnh", q_wide, seen_sums, precision=highest)
    output = numer / denominator[..., None]
    numer_grad = (grad_wide / denominator[..., None]).astype(jnp.bfloat16)
    denom_grad = -jnp.sum(grad_wide * output, axis=-1) / denominator
    q_grad = jnp.einsum(
        "fnhe,fhde->fnhd", numer_grad.astype(jnp.float32), seen_states, precision=highest
    )
    q_grad = (q_grad + denom_grad[..., None] * seen_sums[:, None]) * slopes(
        queries.reshape(head_shape)
    )
    grad_states = jnp.einsum(
        "fnhd,fnhe->fhde", q_feat, numer_grad, preferred_element_type=jnp.float32
    )
    grad_sums = jnp.einsum("fnhd,fnh->fhd", q_wide, denom_grad, precision=highest)
    grad_states, grad_sums = lax.psum((grad_states, grad_sums), "space")
    later = prefix(
        (jnp.sum(grad_states, axis=0), jnp.sum(grad_sums, axis=0)),
        "tm",
        add_pair,
        (
            jnp.zeros(grad_states.shape[1:], jnp.float32),
            jnp.zeros(grad_sums.shape[1:], jnp.float32),
        ),
        True,
    )
    seen_grads = (
        jnp.einsum("fg,fhde->ghde", visible, grad_states, precision=highest) + later[0][None]
    )
    seen_gsums = jnp.einsum("fg,fhd->ghd", visible, grad_sums, precision=highest) + later[1][None]
    k_grad = jnp.einsum(
        "fnhe,fhde->fnhd", v_heads.astype(jnp.float32), seen_grads, precision=highest
    )
    k_grad = (k_grad + seen_gsums[:, None]) * slopes(keys.reshape(head_shape))
    v_grad = jnp.einsum(
        "fnhd,fhde->fnhe", k_feat.astype(jnp.float32), seen_grads, precision=highest
    )
    out_shape = (frames, rows, cols, width)
    padded = jnp.pad(rimmed.astype(jnp.float32), ((0, 0), (0, 0), (1, 1), (0, 0)))
    input_wide = conv_input.astype(jnp.float32)
    accum = jnp.zeros(conv_grad.shape, jnp.float32)
    kernel_rows = []
    for i in range(3):
        for j in range(3):
            window = padded[:, 2 - i : 2 - i + rows, 2 - j : 2 - j + cols]
            accum = accum + conv_weight[3 * i + j] * window
            kernel_rows.append(jnp.sum(window * input_wide, axis=(0, 1, 2)))
    kernel_total = lax.psum(jnp.stack(kernel_rows), ("tm", "space"))
    tokens_all = frames * rows * cols * lax.axis_size("tm") * lax.axis_size("space")
    kernel_grad = kernel_total * (1.0 / math.sqrt(tokens_all))
    return (
        q_grad.astype(jnp.bfloat16).reshape(out_shape),
        k_grad.astype(jnp.bfloat16).reshape(out_shape),
        v_grad.astype(jnp.bfloat16).reshape(out_shape),
        accum.astype(jnp.bfloat16),
        kernel_grad,
    )


def solution(mesh):
    placed = (
        P("tm", "space", None, None),
        P("tm", "space", None, None),
        P("tm", "space", None, None),
        P("tm", "space", None, None),
        P("tm"),
        P("tm", "space", None, None),
        P("tm", "space", None, None),
        P(),
    )
    return jax.shard_map(
        body,
        mesh=mesh,
        in_specs=placed,
        out_specs=(
            P("tm", "space", None, None),
            P("tm", "space", None, None),
            P("tm", "space", None, None),
            P("tm", "space", None, None),
            P(),
        ),
        check_vma=False,
    )
```

profile of v0, /device:TPU:1, one launch (start us, length us, event | category | flops | bytes accessed | tf_op | source)
XLA Modules:
  0.0 849.6 jit_solution(3635706949680957188)
XLA Ops:
  7.2 2.0 reshape.94
  9.2 2.7 convert_reduce_fusion
  12.8 1.9 fusion.78
  14.8 119.5 %all-reduce.5.cloned.1.call-done = f32[2,20,112,112]{3,2,1,0:T(8,128)} async-done(((f32[2,20,112,112]{3,2,1,0:T(8,128)}), f32[2,20,112,112]{3,2,1,0:T(8,128)}) %all-reduce.5.cloned.1.call-update) | async-done | bytes 2007056 | tf_op jit(solution)/shard_map/psum | solution.py:78
  134.3 2.9 reduce_sum.137
  138.6 2.3 collective-permute-start.1
  140.8 3.3 collective-permute-start
  144.4 2.0 reshape.99
  148.6 44.8 %psum.36 = f32[2,20,112]{2,0,1:T(2,128)S(1)} all-reduce(f32[2,20,112]{2,0,1:T(2,128)S(1)} %copy.57), channel_id=1, replica_groups=mesh['tm'=16,'space'=16] {'space'}, use_global_device_ids=true, to_apply=%region_4.5 | all-reduce | flops 4480 | bytes 35840 | tf_op jit(solution)/shard_map/psum | solution.py:78
  193.5 22.7 %all-gather.4 = f32[16,20,112]{2,1,0:T(8,128)} all-gather(f32[1,20,112]{2,1,0:T(8,128)S(1)} %bitcast.88), channel_id=3, replica_groups=mesh['tm'=16,'space'=16] {'tm'}, dimensions={0}, use_global_device_ids=true | all-gather | bytes 152320 | tf_op jit(solution)/shard_map/all_gather | solution.py:33
  216.2 47.2 %all-gather.9.cloned.1.call-done = f32[320,112,112]{2,1,0:T(8,128)} async-done(((f32[20,112,112]{2,1,0:T(8,128)}), f32[320,112,112]{2,1,0:T(8,128)}) %all-gather.9.cloned.1.call-update) | async-done | bytes 16056336 | tf_op jit(solution)/shard_map/all_gather | solution.py:33
  264.9 3.7 fusion.82
  268.8 1.9 maximum_convert_fusion
  270.7 3.6 fusion.8
  274.5 1.6 stack.39
  276.4 140.1 %all-reduce.7.cloned.1.call-done = f32[2,20,112,112]{3,2,1,0:T(8,128)} async-done(((f32[2,20,112,112]{3,2,1,0:T(8,128)}), f32[2,20,112,112]{3,2,1,0:T(8,128)}) %all-reduce.7.cloned.1.call-update) | async-done | bytes 2007056 | tf_op jit(solution)/shard_map/psum | solution.py:105
  416.5 3.0 reduce_sum.142
  419.5 1.9 select_n.43
  421.4 1.9 select_n.45
  423.9 12.4 %add_convert_fusion = bf16[2,2,32,5632]{3,2,1,0:T(8,128)(2,1)} fusion(f32[2,4,32,5632]{3,2,1,0:T(8,128)} %copy-done, f32[5632]{0:T(1024)S(1)} %get-tuple-element.140, f32[5632]{0:T(1024)S(1)} %get-tuple-element.141, f32[5632]{0:T(1024)S(1)} %get-tuple-element.134, f32[5632]{0:T(1024)S(1)} %get-tuple-element.135, f32[5632]{0:T(1024)S(1)} %get-tuple-element.136, ...), kind=kLoop, calls=%fused_computation.29 | loop fusion | flops 12976128 | bytes 16062464 | tf_op jit(solution)/shard_map/convert_element_type | solution.py:144
  436.3 233.9 %all-reduce.9.cloned.1.call-done = f32[9,5632]{1,0:T(8,128)} async-done(((f32[9,5632]{1,0:T(8,128)}), f32[9,5632]{1,0:T(8,128)}) %all-reduce.9.cloned.1.call-update) | async-done | bytes 202768 | tf_op jit(solution)/shard_map/psum | solution.py:137
  670.2 1.8 broadcast_multiply_fusion
  672.0 6.7 fusion.48
  678.7 1.6 fusion.66
  680.4 2.8 fusion.54
  683.6 1.4 reshape.96
  685.7 44.5 %psum.38 = f32[2,20,112]{2,0,1:T(2,128)S(1)} all-reduce(f32[2,20,112]{2,0,1:T(2,128)S(1)} %bitcast.87), channel_id=1, replica_groups=mesh['tm'=16,'space'=16] {'space'}, use_global_device_ids=true, to_apply=%region_11.12 | all-reduce | flops 4480 | bytes 35840 | tf_op jit(solution)/shard_map/psum | solution.py:105
  730.2 22.3 %all-gather.5 = f32[16,20,112]{2,1,0:T(8,128)} all-gather(f32[1,20,112]{2,1,0:T(8,128)S(1)} %bitcast.89), channel_id=5, replica_groups=mesh['tm'=16,'space'=16] {'tm'}, dimensions={0}, use_global_device_ids=true | all-gather | bytes 152320 | tf_op jit(solution)/shard_map/all_gather | solution.py:33
  752.5 43.3 %all-gather.11.cloned.1.call-done = f32[320,112,112]{2,1,0:T(8,128)} async-done(((f32[20,112,112]{2,1,0:T(8,128)}), f32[320,112,112]{2,1,0:T(8,128)}) %all-gather.11.cloned.1.call-update) | async-done | bytes 16056336 | tf_op jit(solution)/shard_map/all_gather | solution.py:33
  795.9 33.4 %while.27 = (s32[]{:T(128)}, f32[20,112,112]{2,1,0:T(8,128)S(1)}, f32[20,112]{1,0:T(8,128)S(1)}, s32[]{:T(128)}, f32[16,20,112,112]{3,2,1,0:T(8,128)}, /*index=5...) while((s32[]{:T(128)}, f32[20,112,112]{2,1,0:T(8,128)S(1)}, ...), condition=%wide.region_14.15_spmd, body=%wide.region_13.14_spmd.sunk | while | flops 253126 | bytes 3037603 | solution.py:42
  796.0 1.6 bitcast_add_fusion.10
  798.3 1.5 bitcast_add_fusion.10
  800.5 1.5 bitcast_add_fusion.10
  802.8 1.5 bitcast_add_fusion.10
  805.0 1.5 bitcast_add_fusion.10
  807.2 1.5 bitcast_add_fusion.10
  809.4 1.5 bitcast_add_fusion.10
  811.6 1.5 bitcast_add_fusion.10
  813.8 1.5 bitcast_add_fusion.10
  816.1 1.5 bitcast_add_fusion.10
  818.3 1.5 bitcast_add_fusion.10
  820.5 1.5 bitcast_add_fusion.10
  822.7 1.5 bitcast_add_fusion.10
  824.9 1.5 bitcast_add_fusion.10
  827.1 1.5 bitcast_add_fusion.10
  829.6 5.5 fusion.51
  836.8 2.5 fusion.57
  841.6 1.4 reshape.98
  (112 shorter events, 23.4 us)
Async XLA Ops:
  7.2 127.1 %all-reduce.5.cloned.1.call-start = ((), (), s32[]{:S(2)}) async-start(), calls=%async_computation | async-start | bytes 4587520 | tf_op jit(solution)/shard_map/psum | solution.py:78
  9.2 5.5 copy-start.4
  12.8 1.9 copy-start.6
  14.8 122.6 %copy-start.3 = (bf16[2,2,32,5632]{3,2,1,0:T(8,128)(2,1)S(1)}, bf16[2,2,32,5632]{3,2,1,0:T(8,128)(2,1)}, u32[]{:S(2)}) copy-start(bf16[2,2,32,5632]{3,2,1,0:T(8,128)(2,1)} %param.18) | copy-start | bytes 4325380
  14.8 248.6 %all-gather.9.cloned.1.call-start = ((), (), s32[]{:S(2)}) async-start(), calls=%async_computation.3 | async-start | bytes 19496960 | tf_op jit(solution)/shard_map/all_gather | solution.py:33
  137.2 7.0 copy-start.22
  137.2 7.2 copy-start.17
  137.3 9.2 %copy-start.18 = (bf16[2,2,32,2240]{3,2,1,0:T(8,128)(2,1)S(1)}, bf16[2,2,32,2240]{3,2,1,0:T(8,128)(2,1)}, u32[]{:S(2)}) copy-start(bf16[2,2,32,2240]{3,2,1,0:T(8,128)(2,1)} %param.12) | copy-start | bytes 1720324
  137.3 279.2 %all-reduce.7.cloned.1.call-start = ((), (), s32[]{:S(2)}) async-start(), calls=%async_computation.1 | async-start | bytes 4587520 | tf_op jit(solution)/shard_map/psum | solution.py:105
  138.6 130.2 %collective-permute-start.1 = (bf16[2,1,32,5632]{3,2,1,0:T(8,128)(2,1)}, bf16[2,1,32,5632]{3,2,1,0:T(8,128)(2,1)}, u32[]{:S(2)}, u32[]{:S(2)}) collective-permute-start(bf16[2,1,32,5632]{3,2,1,0:T(8,128)(2,1)} %get-tuple-element.169), channel_id=1, source_target_pairs={{1,0},{2,1},{3,2},{4,3},{5,4},{6,5},{7,6},{8,7},{9,8},{10,9},{11,1... | collective-permute-start | bytes 2162696 | tf_op jit(solution)/shard_map/ppermute | solution.py:22
  140.8 127.9 %collective-permute-start = (bf16[2,1,32,5632]{3,2,1,0:T(8,128)(2,1)}, bf16[2,1,32,5632]{3,2,1,0:T(8,128)(2,1)}, u32[]{:S(2)}, u32[]{:S(2)}) collective-permute-start(bf16[2,1,32,5632]{3,2,1,0:T(8,128)(2,1)} %get-tuple-element.168), channel_id=1, source_target_pairs={{0,1},{1,2},{2,3},{3,4},{4,5},{5,6},{6,7},{7,8},{8,9},{9,10},{10,1... | collective-permute-start | bytes 2162696 | tf_op jit(solution)/shard_map/ppermute | solution.py:20
  148.6 116.3 %copy-start.14 = (bf16[2,64,20,112]{3,2,1,0:T(8,128)(2,1)}, bf16[2,64,20,112]{3,2,1,0:T(8,128)(2,1)S(1)}, u32[]{:S(2)}) copy-start(bf16[2,64,20,112]{3,2,1,0:T(8,128)(2,1)S(1)} %reshape.95) | copy-start | bytes 1720324
  263.8 4.8 copy-start.20
  268.7 401.5 %all-reduce.9.cloned.1.call-start = ((), (), s32[]{:S(2)}) async-start(), calls=%async_computation.2 | async-start | bytes 720896 | tf_op jit(solution)/shard_map/psum | solution.py:137
  268.7 1.9 copy-start.13
  270.6 3.6 copy-start
  276.2 143.3 %copy-start.9 = (f32[2,2,32,2240]{3,2,1,0:T(8,128)S(1)}, f32[2,2,32,2240]{3,2,1,0:T(8,128)}, u32[]{:S(2)}) copy-start(f32[2,2,32,2240]{3,2,1,0:T(8,128)} %get-tuple-element.172) | copy-start | bytes 3440644
  276.2 519.6 %all-gather.11.cloned.1.call-start = ((), (), s32[]{:S(2)}) async-start(), calls=%async_computation.4 | async-start | bytes 19496960 | tf_op jit(solution)/shard_map/all_gather | solution.py:33
  419.5 1.9 copy-start.10
  421.4 1.9 copy-start.19
  423.8 248.1 %copy-start.21 = (f32[2,20,112]{2,0,1:T(2,128)S(1)}, f32[2,20,112]{2,0,1:T(2,128)}, u32[]{:S(2)}) copy-start(f32[2,20,112]{2,0,1:T(2,128)} %copy-done.20) | copy-start | bytes 53764
  423.8 248.1 %copy-start.1 = (f32[2,20,112,112]{3,2,1,0:T(8,128)S(1)}, f32[2,20,112,112]{3,2,1,0:T(8,128)}, u32[]{:S(2)}) copy-start(f32[2,20,112,112]{3,2,1,0:T(8,128)} %all-reduce.5.cloned.1.call-done) | copy-start | bytes 6021124
  671.9 6.7 copy-start.11
  671.9 6.7 copy-start.15
  678.7 1.7 copy-start.12
  683.1 1.9 copy-start.16
  795.9 33.7 %copy-start.2 = (f32[2,20,112,112]{3,2,1,0:T(8,128)S(1)}, f32[2,20,112,112]{3,2,1,0:T(8,128)}, u32[]{:S(2)}) copy-start(f32[2,20,112,112]{3,2,1,0:T(8,128)} %all-reduce.7.cloned.1.call-done) | copy-start | bytes 6021124
  829.6 5.6 copy-start.7
  835.2 1.3 copy-start.5
  835.2 1.6 copy-start.8
Sparse Core Ops, SparseCore 0:
  14.9 119.3 all-reduce.4
  137.4 125.9 all-gather.8
  268.8 147.6 all-reduce.6
  422.5 247.6 all-reduce.8
  672.5 123.2 all-gather.10
where the time goes:
time: 851 us; the launch traced here: 850 us
  waiting for transfers between devices  584 us (69%)
  blocking collectives  134 us (16%)
  other arithmetic  63.2 us (7%)
  matrix products  28.2 us (3%)
  local copies, waits for them, and re-layouts  19.3 us (2%)
  between operations  14.3 us (2%)
    psum x1, waiting for transfers between devices, body(): kernel_total = lax.psum(jnp.stack(kernel_rows), ('tm', 'space'))  234 us
    psum x1, waiting for transfers between devices, body(): grad_states, grad_sums = lax.psum((grad_states, grad_sums), 'space')  140 us
    psum x1, waiting for transfers between devices, body(): states, sums = lax.psum((states, sums), 'space')  119 us
    all_gather x2, waiting for transfers between devices, prefix(): gathered = jax.tree.map(lambda a: lax.all_gather(a, axis), part)  90.5 us
    all_gather x2, blocking collectives, prefix(): gathered = jax.tree.map(lambda a: lax.all_gather(a, axis), part)  45 us
    psum x1, blocking collectives, body(): states, sums = lax.psum((states, sums), 'space')  44.8 us
    psum x1, blocking collectives, body(): grad_states, grad_sums = lax.psum((grad_states, grad_sums), 'space')  44.5 us
    add x30, other arithmetic, add_pair(): return (earlier[0] + later[0], earlier[1] + later[1])  33.3 us
  transfers between devices with their start and end apart: 7, of which 5 were waited for; matrix products, arithmetic and copies ran while one was open for 6% of the time, Pallas kernels for 0%

commit v1 on v0

--- a/solution.py
+++ b/solution.py
@@ -134,7 +134,9 @@
             window = padded[:, 2 - i : 2 - i + rows, 2 - j : 2 - j + cols]
             accum = accum + conv_weight[3 * i + j] * window
             kernel_rows.append(jnp.sum(window * input_wide, axis=(0, 1, 2)))
-    kernel_total = lax.psum(jnp.stack(kernel_rows), ("tm", "space"))
+    kernel_total = jnp.stack(kernel_rows)
+    for h in ("space", "tm"):
+        kernel_total = lax.psum(kernel_total, axis_name=h)
     tokens_all = frames * rows * cols * lax.axis_size("tm") * lax.axis_size("space")
     kernel_grad = kernel_total * (1.0 / math.sqrt(tokens_all))
     return (

time: 851 us -> 688 us (0.81)
  waiting for transfers between devices: 584 us -> 418 us
    psum x1, waiting for transfers between devices: 234 us -> 0.01 us  [body(): kernel_total = lax.psum(kernel_total, axis_name=h)]
    all_gather x2, waiting for transfers between devices: 90.5 us -> 160 us  [prefix(): gathered = jax.tree.map(lambda a: lax.all_gather(a, axis), part)]
  transfers between devices with their start and end apart: 7 -> 7, of which waited for: 5 -> 4; matrix products, arithmetic and copies ran while one was open for 6% -> 7% of each run, Pallas kernels for 0% -> 0%
where the time goes in v1:
time: 688 us; the launch traced here: 686 us
  waiting for transfers between devices  418 us (61%)
  blocking collectives  136 us (20%)
  other arithmetic  63.3 us (9%)
  matrix products  28.2 us (4%)
  local copies, waits for them, and re-layouts  20.9 us (3%)
  between operations  14.3 us (2%)
    all_gather x2, waiting for transfers between devices, prefix(): gathered = jax.tree.map(lambda a: lax.all_gather(a, axis), part)  160 us
    psum x1, waiting for transfers between devices, body(): grad_states, grad_sums = lax.psum((grad_states, grad_sums), 'space')  138 us
    psum x1, waiting for transfers between devices, body(): states, sums = lax.psum((states, sums), 'space')  119 us
    psum x1, blocking collectives, body(): states, sums = lax.psum((states, sums), 'space')  47.3 us
    psum x1, blocking collectives, body(): grad_states, grad_sums = lax.psum((grad_states, grad_sums), 'space')  46.7 us
    all_gather x2, blocking collectives, prefix(): gathered = jax.tree.map(lambda a: lax.all_gather(a, axis), part)  41.5 us
    add x30, other arithmetic, add_pair(): return (earlier[0] + later[0], earlier[1] + later[1])  33.3 us
  transfers between devices with their start and end apart: 7, of which 4 were waited for; matrix products, arithmetic and copies ran while one was open for 7% of the time, Pallas kernels for 0%

profile of v1, /device:TPU:1, one launch (start us, length us, event | category | flops | bytes accessed | tf_op | source)
XLA Modules:
  0.0 686.2 jit_solution(3723952258673597654)
XLA Ops:
  7.2 2.0 reshape.94
  9.2 2.7 convert_reduce_fusion
  12.8 1.9 fusion.78
  14.8 119.5 %all-reduce.6.cloned.1.call-done = f32[2,20,112,112]{3,2,1,0:T(8,128)} async-done(((f32[2,20,112,112]{3,2,1,0:T(8,128)}), f32[2,20,112,112]{3,2,1,0:T(8,128)}) %all-reduce.6.cloned.1.call-update) | async-done | bytes 2007056 | tf_op jit(solution)/shard_map/psum | solution.py:78
  134.3 3.0 reduce_sum.137
  138.5 1.9 collective-permute-start
  140.5 3.3 collective-permute-start.1
  143.9 1.9 reshape.99
  147.2 1.7 reshape.95
  149.0 47.3 %psum.43 = f32[2,20,112]{2,0,1:T(2,128)S(1)} all-reduce(f32[2,20,112]{2,0,1:T(2,128)S(1)} %copy.57), channel_id=1, replica_groups=mesh['tm'=16,'space'=16] {'space'}, use_global_device_ids=true, to_apply=%region_4.5 | all-reduce | flops 4480 | bytes 35840 | tf_op jit(solution)/shard_map/psum | solution.py:78
  196.4 21.1 %all-gather.4 = f32[16,20,112]{2,1,0:T(8,128)S(1)} all-gather(f32[1,20,112]{2,1,0:T(8,128)S(1)} %bitcast.88), channel_id=3, replica_groups=mesh['tm'=16,'space'=16] {'tm'}, dimensions={0}, use_global_device_ids=true | all-gather | bytes 152320 | tf_op jit(solution)/shard_map/all_gather | solution.py:33
  217.6 1.9 maximum_convert_fusion
  219.5 3.6 fusion.8
  223.3 1.6 stack.39
  225.0 38.5 %all-gather.9.cloned.1.call-done = f32[320,112,112]{2,1,0:T(8,128)} async-done(((f32[20,112,112]{2,1,0:T(8,128)}), f32[320,112,112]{2,1,0:T(8,128)}) %all-gather.9.cloned.1.call-update) | async-done | bytes 16056336 | tf_op jit(solution)/shard_map/all_gather | solution.py:33
  265.7 3.7 fusion.82
  269.5 138.4 %all-reduce.10.cloned.1.call-done = (f32[2,20,112,112]{3,2,1,0:T(8,128)}, f32[9,5632]{1,0:T(8,128)}) async-done(((f32[2,20,112,112]{3,2,1,0:T(8,128)}, f32[9,5632]{1,0:T(8,128)}), (f32[2,20,112,112]{3,2,1,0:T(8,128)}, f32[9,5632]{1,0:T(8,128)})) %all-reduce.10.cloned.1.call-update) | async-done | bytes 2209808 | tf_op jit(solution)/shard_map/psum | solution.py:105
  408.2 3.0 reduce_sum.142
  411.2 1.9 select_n.43
  413.1 2.0 select_n.45
  415.6 12.4 %add_convert_fusion = bf16[2,2,32,5632]{3,2,1,0:T(8,128)(2,1)} fusion(f32[2,4,32,5632]{3,2,1,0:T(8,128)} %copy-done, f32[5632]{0:T(1024)S(1)} %get-tuple-element.140, f32[5632]{0:T(1024)S(1)} %get-tuple-element.141, f32[5632]{0:T(1024)S(1)} %get-tuple-element.134, f32[5632]{0:T(1024)S(1)} %get-tuple-element.135, f32[5632]{0:T(1024)S(1)} %get-tuple-element.136, ...), kind=kLoop, calls=%fused_computation.29 | loop fusion | flops 12976128 | bytes 16062464 | tf_op jit(solution)/shard_map/convert_element_type | solution.py:146
  428.1 6.7 fusion.48
  434.8 1.6 fusion.66
  437.1 2.8 fusion.54
  440.3 1.4 reshape.96
  441.7 46.7 %psum.45 = f32[2,20,112]{2,0,1:T(2,128)S(1)} all-reduce(f32[2,20,112]{2,0,1:T(2,128)S(1)} %bitcast.87), channel_id=1, replica_groups=mesh['tm'=16,'space'=16] {'space'}, use_global_device_ids=true, to_apply=%region_11.12 | all-reduce | flops 4480 | bytes 35840 | tf_op jit(solution)/shard_map/psum | solution.py:105
  488.5 20.3 %all-gather.5 = f32[16,20,112]{2,1,0:T(8,128)} all-gather(f32[1,20,112]{2,1,0:T(8,128)S(1)} %bitcast.89), channel_id=5, replica_groups=mesh['tm'=16,'space'=16] {'tm'}, dimensions={0}, use_global_device_ids=true | all-gather | bytes 152320 | tf_op jit(solution)/shard_map/all_gather | solution.py:33
  508.8 1.8 broadcast_multiply_fusion
  510.6 121.6 %all-gather.11.cloned.1.call-done = f32[320,112,112]{2,1,0:T(8,128)} async-done(((f32[20,112,112]{2,1,0:T(8,128)}), f32[320,112,112]{2,1,0:T(8,128)}) %all-gather.11.cloned.1.call-update) | async-done | bytes 16056336 | tf_op jit(solution)/shard_map/all_gather | solution.py:33
  632.3 33.7 %while.27 = (s32[]{:T(128)}, f32[20,112,112]{2,1,0:T(8,128)S(1)}, f32[20,112]{1,0:T(8,128)S(1)}, s32[]{:T(128)}, f32[16,20,112,112]{3,2,1,0:T(8,128)}, /*index=5...) while((s32[]{:T(128)}, f32[20,112,112]{2,1,0:T(8,128)S(1)}, ...), condition=%wide.region_14.15_spmd, body=%wide.region_13.14_spmd.sunk | while | flops 253126 | bytes 3037603 | solution.py:42
  633.2 1.5 bitcast_add_fusion.10
  635.4 1.5 bitcast_add_fusion.10
  637.7 1.5 bitcast_add_fusion.10
  639.9 1.5 bitcast_add_fusion.10
  642.1 1.5 bitcast_add_fusion.10
  644.4 1.5 bitcast_add_fusion.10
  646.6 1.5 bitcast_add_fusion.10
  648.8 1.5 bitcast_add_fusion.10
  651.1 1.5 bitcast_add_fusion.10
  653.3 1.5 bitcast_add_fusion.10
  655.5 1.5 bitcast_add_fusion.10
  657.8 1.5 bitcast_add_fusion.10
  660.0 1.5 bitcast_add_fusion.10
  662.2 1.5 bitcast_add_fusion.10
  664.5 1.5 bitcast_add_fusion.10
  666.2 5.5 fusion.51
  673.4 2.5 fusion.57
  678.3 1.4 reshape.98
  (106 shorter events, 23.5 us)
Async XLA Ops:
  7.2 127.1 %all-reduce.6.cloned.1.call-start = ((), (), s32[]{:S(2)}) async-start(), calls=%async_computation | async-start | bytes 4587520 | tf_op jit(solution)/shard_map/psum | solution.py:78
  9.2 5.5 copy-start.4
  12.8 1.9 copy-start.6
  14.8 122.6 %copy-start.3 = (bf16[2,2,32,5632]{3,2,1,0:T(8,128)(2,1)S(1)}, bf16[2,2,32,5632]{3,2,1,0:T(8,128)(2,1)}, u32[]{:S(2)}) copy-start(bf16[2,2,32,5632]{3,2,1,0:T(8,128)(2,1)} %param.18) | copy-start | bytes 4325380
  14.8 248.6 %all-gather.9.cloned.1.call-start = ((), (), s32[]{:S(2)}) async-start(), calls=%async_computation.2 | async-start | bytes 19496960 | tf_op jit(solution)/shard_map/all_gather | solution.py:33
  137.2 6.5 copy-start.19
  137.2 6.7 copy-start.15
  137.3 270.7 %all-reduce.10.cloned.1.call-start = ((), (), s32[]{:S(2)}) async-start(), calls=%async_computation.4 | async-start | bytes 5308416 | tf_op jit(solution)/shard_map/psum | solution.py:105
  138.5 79.0 %collective-permute-start = (bf16[2,1,32,5632]{3,2,1,0:T(8,128)(2,1)}, bf16[2,1,32,5632]{3,2,1,0:T(8,128)(2,1)}, u32[]{:S(2)}, u32[]{:S(2)}) collective-permute-start(bf16[2,1,32,5632]{3,2,1,0:T(8,128)(2,1)} %get-tuple-element.170), channel_id=1, source_target_pairs={{0,1},{1,2},{2,3},{3,4},{4,5},{5,6},{6,7},{7,8},{8,9},{9,10},{10,1... | collective-permute-start | bytes 2162696 | tf_op jit(solution)/shard_map/ppermute | solution.py:20
  140.5 77.1 %collective-permute-start.1 = (bf16[2,1,32,5632]{3,2,1,0:T(8,128)(2,1)}, bf16[2,1,32,5632]{3,2,1,0:T(8,128)(2,1)}, u32[]{:S(2)}, u32[]{:S(2)}) collective-permute-start(bf16[2,1,32,5632]{3,2,1,0:T(8,128)(2,1)} %get-tuple-element.171), channel_id=1, source_target_pairs={{1,0},{2,1},{3,2},{4,3},{5,4},{6,5},{7,6},{8,7},{9,8},{10,9},{11,1... | collective-permute-start | bytes 2162696 | tf_op jit(solution)/shard_map/ppermute | solution.py:22
  217.5 1.9 copy-start.12
  219.4 3.6 copy-start
  263.5 1.1 copy-start.13
  263.8 5.6 copy-start.17
  269.5 239.4 %all-reduce.8.cloned.1.call-start = ((), (), s32[]{:S(2)}) async-start(), calls=%async_computation.1 | async-start | bytes 720896 | tf_op jit(solution)/shard_map/psum | solution.py:139
  408.0 224.3 %all-gather.11.cloned.1.call-start = ((), (), s32[]{:S(2)}) async-start(), calls=%async_computation.3 | async-start | bytes 19496960 | tf_op jit(solution)/shard_map/all_gather | solution.py:33
  411.2 1.9 copy-start.9
  413.1 2.0 copy-start.16
  415.6 12.4 %copy-start.18 = (f32[2,20,112]{2,0,1:T(2,128)S(1)}, f32[2,20,112]{2,0,1:T(2,128)}, u32[]{:S(2)}) copy-start(f32[2,20,112]{2,0,1:T(2,128)} %copy-done.17) | copy-start | bytes 53764
  415.6 12.4 %copy-start.1 = (f32[2,20,112,112]{3,2,1,0:T(8,128)S(1)}, f32[2,20,112,112]{3,2,1,0:T(8,128)}, u32[]{:S(2)}) copy-start(f32[2,20,112,112]{3,2,1,0:T(8,128)} %all-reduce.6.cloned.1.call-done) | copy-start | bytes 6021124
  428.0 6.7 copy-start.10
  428.1 6.7 copy-start.14
  434.8 2.3 copy-start.11
  632.3 33.9 %copy-start.2 = (f32[2,20,112,112]{3,2,1,0:T(8,128)S(1)}, f32[2,20,112,112]{3,2,1,0:T(8,128)}, u32[]{:S(2)}) copy-start(f32[2,20,112,112]{3,2,1,0:T(8,128)} %get-tuple-element.166) | copy-start | bytes 6021124
  666.2 5.6 copy-start.7
  671.8 1.3 copy-start.5
  671.8 1.6 copy-start.8
Sparse Core Ops, SparseCore 0:
  14.9 119.3 all-reduce.5
  137.4 125.9 all-gather.8
  269.6 138.2 all-reduce.9
  411.4 93.6 all-reduce.7
  507.7 124.4 all-gather.10
